TPU v7x, 128 devices: a whole 4x4x4 slice. The times are simulated.
128 devices in a mesh: sect: 4 (over y_lo, core), tile: 32 (over x, y_hi, z).
Axes of the slice: x: 4, y: 4 (y_hi: 2, y_lo: 2; y = y_hi * 2 + y_lo), z: 4, core: 2. Of those that a mesh axis runs over, the one named last changes fastest.
Arguments:
- tracer_values: float32 [4, 16, 512, 3584], P('sect', None, 'tile'), may hold values from -6 to 6
- courant_numbers: bfloat16 [2, 4, 16, 512, 3584], P(None, 'sect', None, 'tile'), may hold values from -0.29882812 to 0.29882812
- diffusion_numbers: bfloat16 [4, 16, 512, 3584], P('sect', None, 'tile'), may hold values from 0.049804688 to 0.19921875
- water_indicator: int32 [512, 3584], P('tile'), may hold values 0 or 1
- downward_lane_pairs: int32 [4, 32, 2, 32, 4], P('sect', 'tile'), may hold values from 0 to 447
- downward_lane_number: int32 [4, 32, 32], P('sect', 'tile'), may hold values from 0 to 4, as said below
- downward_patch_matrix: bfloat16 [4, 32, 32, 4, 128, 128], P('sect', 'tile'), may hold values from -0.5 to 0.5
- upward_lane_pairs: int32 [4, 32, 2, 32, 4], P('sect', 'tile'), may hold values from 0 to 447
- upward_lane_number: int32 [4, 32, 32], P('sect', 'tile'), may hold values from 0 to 4, as said below
- upward_patch_matrix: bfloat16 [4, 32, 32, 4, 128, 128], P('sect', 'tile'), may hold values from -0.5 to 0.5
Outputs:
- advanced: float32 [4, 16, 512, 3584], P('sect', None, 'tile')
Inputs may be any that keep to these rules, and one draw needn't show every extreme that they name: `downward_lane_number`: zero on section 3; in every draw one ocean tile has 4 live slots from every atmosphere device. `upward_lane_number`: zero on section 3; in every draw one ocean tile fills 4 slots of every atmosphere device.
All inputs are finite; a program needn't handle non-finite values. No bound on the sum of `water_indicator` on one device may be relied on, other than what follows from the above.
Results may differ from a plain program's by a relative error of at most 0.00032.
Values may be sent and summed in bfloat16 or wider, within the bound.
A program may use at most 128 MiB of HBM per device.

v0:
```python
import jax
import jax.numpy as jnp
from jax import lax
from jax.sharding import PartitionSpec as P

SUBSTEPS = 3


def from_root(block, axis, source):
    block = jnp.where(lax.axis_index(axis) == source, block, jnp.zeros_like(block))
    return lax.psum(block, axis)


def with_halo(cells, sides, width):
    for axis, dim in sides:
        count = lax.axis_size(axis)
        ends = count - 1
        head = lax.slice_in_dim(cells, 0, width, axis=dim)
        tail = lax.slice_in_dim(cells, cells.shape[dim] - width, cells.shape[dim], axis=dim)
        cells = jnp.concatenate(
            [
                lax.ppermute(tail, axis, [(i, (i + 1) % count) for i in range(ends)]),
                cells,
                lax.ppermute(head, axis, [((i + 1) % count, i) for i in range(ends)]),
            ],
            axis=dim,
        )
    return cells


def stencil(padded, wind_east, wind_north, mixing_now, wet_mask):
    centre = padded[..., 1:-1, :]
    upper_row = padded[..., :-2, :]
    lower_row = padded[..., 2:, :]
    widened = jnp.pad(centre, [(0, 0)] * (centre.ndim - 1) + [(1, 1)])
    right_col = widened[..., 2:]
    left_col = widened[..., :-2]
    updated = (
        centre
        - 0.5 * wind_east * (right_col - left_col)
        - 0.5 * wind_north * (lower_row - upper_row)
        + mixing_now * (right_col + left_col + upper_row + lower_row - 4.0 * centre)
    )
    return updated * wet_mask


def accumulate(target_ids, values, count_of_blocks):
    flat_ids = target_ids.reshape(-1)
    onehot = (flat_ids[None, :] == jnp.arange(count_of_blocks, dtype=jnp.int32)[:, None]).astype(
        jnp.bfloat16
    )
    return jnp.dot(
        onehot,
        values.reshape(flat_ids.shape[0], values.shape[-1]),
        preferred_element_type=jnp.float32,
    )


def per_device(
    tracer_values,
    courant_numbers,
    diffusion_numbers,
    water_indicator,
    downward_lane_pairs,
    downward_lane_number,
    downward_patch_matrix,
    upward_lane_pairs,
    upward_lane_number,
    upward_patch_matrix,
):
    field = tracer_values[0]
    depth_levels, rows, columns = field.shape
    cells_per_block = downward_patch_matrix.shape[-1]
    count_of_blocks = rows * columns // cells_per_block
    tiles = downward_lane_number.shape[-1]
    capacity = downward_lane_pairs.shape[-1]
    partition_sum = lax.axis_size("sect")
    ocean = lax.axis_index("sect") == partition_sum - 1
    is_ocean = ocean.astype(jnp.float32)
    water_indicator_real = water_indicator.astype(jnp.float32)
    lane_labels = jnp.arange(capacity, dtype=jnp.int32)[None, :]
    bottom = field[0].astype(jnp.bfloat16).reshape(count_of_blocks, cells_per_block)
    active = lane_labels < downward_lane_number[0, 0][:, None]
    selected_blocks = bottom[downward_lane_pairs[0, 0, 0]]
    products = jnp.einsum(
        "hgw,hgwy->hgy",
        selected_blocks,
        downward_patch_matrix[0, 0],
        preferred_element_type=jnp.float32,
    )
    products = jnp.where(active[..., None], products, 0.0).astype(jnp.bfloat16)
    target_ids = jnp.where(active, downward_lane_pairs[0, 0, 1], -1)
    arrived, arrived_ids = (
        lax.all_to_all(products, "tile", split_axis=0, concat_axis=0, tiled=True),
        lax.all_to_all(target_ids, "tile", split_axis=0, concat_axis=0, tiled=True),
    )
    partial_value = accumulate(arrived_ids, arrived, count_of_blocks)
    ocean_flux = lax.psum(partial_value, "sect")
    flux_field = ocean_flux.reshape(rows, columns)
    surface_level = field[0] + is_ocean * flux_field * water_indicator_real
    heat_patches = (
        (surface_level * water_indicator_real)
        .astype(jnp.bfloat16)
        .reshape(count_of_blocks, cells_per_block)
    )
    shard_heat_field = from_root(heat_patches, "sect", partition_sum - 1)
    sender_labels = upward_lane_pairs[0, 0, 0]
    entire_heat_field = lax.all_gather(shard_heat_field, "tile", axis=0, tiled=True)
    initial_shifts = jnp.arange(tiles, dtype=jnp.int32)[:, None] * count_of_blocks
    collected_patches = entire_heat_field[initial_shifts + sender_labels]
    incoming_patches = jnp.einsum(
        "hgw,hgwy->hgy",
        collected_patches,
        upward_patch_matrix[0, 0],
        preferred_element_type=jnp.float32,
    )
    upward_lane_live = lane_labels < upward_lane_number[0, 0][:, None]
    incoming_patches = jnp.where(upward_lane_live[..., None], incoming_patches, 0.0)
    upward_lane_labels = jnp.where(upward_lane_live, upward_lane_pairs[0, 0, 1], -1).reshape(-1)
    onehot_back = (
        upward_lane_labels[None, :] == jnp.arange(count_of_blocks, dtype=jnp.int32)[:, None]
    ).astype(jnp.float32)
    air_patch_lines = jnp.dot(
        onehot_back,
        incoming_patches.reshape(upward_lane_labels.shape[0], cells_per_block),
        precision=lax.Precision.HIGHEST,
        preferred_element_type=jnp.float32,
    )
    surface_level = surface_level + 0.5 * air_patch_lines.reshape(rows, columns)
    field = field.at[0].set(surface_level)
    wet_mask = jnp.where(ocean, water_indicator_real, 1.0)[None]
    wind_east = courant_numbers[0, 0].astype(jnp.float32)
    wind_north = courant_numbers[1, 0].astype(jnp.float32)
    mixing_now = diffusion_numbers[0].astype(jnp.float32)
    for substep in range(SUBSTEPS):
        padded = with_halo(field, (("tile", 1),), 1)
        field = stencil(padded, wind_east, wind_north, mixing_now, wet_mask)
    return field[None]


def solution(mesh):
    placed = (
        P("sect", None, "tile", None),
        P(None, "sect", None, "tile", None),
        P("sect", None, "tile", None),
        P("tile", None),
        P("sect", "tile", None, None, None),
        P("sect", "tile", None),
        P("sect", "tile", None, None, None, None),
        P("sect", "tile", None, None, None),
        P("sect", "tile", None),
        P("sect", "tile", None, None, None, None),
    )
    return jax.shard_map(
        per_device,
        mesh=mesh,
        in_specs=placed,
        out_specs=P("sect", None, "tile", None),
        check_vma=False,
    )
```

profile of v0, /device:TPU:6, one launch (start us, length us, event | category | flops | bytes accessed | tf_op | source)
XLA Modules:
  0.0 281.7 jit_solution(12068850138414625184)
XLA Ops:
  6.5 0.7 bitcast_select_fusion
  7.3 0.7 copy.19
  8.0 11.1 %all-to-all-start = ((s32[32,1,4]{2,1,0:T(1,128)}), s32[32,1,4]{2,1,0:T(1,128)S(1)}, u32[]{:S(2)}, u32[]{:S(2)}) async-start(s32[32,1,4]{2,1,0:T(1,128)} %copy.19), calls=%async_computation | async-start | bytes 32768 | tf_op jit(solution)/shard_map/all_to_all | solution.py:95
  19.0 0.7 compare_select_fusion.1
  19.7 0.7 iota_compare_fusion.5
  20.5 0.1 reshape.261
  20.7 1.0 slice.159
  21.6 0.2 convert_element_type.41
  21.8 0.7 gather_fusion
  22.5 3.4 %fusion.2 = f32[32,4,1,128]{3,2,1,0:T(1,128)S(1)} fusion(bf16[1,1,32,4,128,128]{5,4,3,2,1,0:T(8,128)(2,1)} %param.18, bf16[32,4,128,1]{2,1,0,3:T(4,128)(2,1)S(1)} %bitcast.87), kind=kOutput, calls=%fused_computation.7 | convolution fusion | flops 4194304 | bytes 4292608 | tf_op jit(solution)/shard_map/hgw,hgwy->hgy/dot_general | solution.py:85
  25.9 0.7 select_convert_fusion
  26.7 0.3 all-to-all-done
  26.9 9.5 %all-to-all-start.1 = ((bf16[32,4,128]{2,1,0:T(4,128)(2,1)}), bf16[32,4,128]{2,1,0:T(4,128)(2,1)S(1)}, u32[]{:S(2)}, u32[]{:S(2)}) async-start(bf16[32,4,128]{2,1,0:T(4,128)(2,1)} %select_convert_fusion), calls=%async_computation.1 | async-start | bytes 65536 | tf_op jit(solution)/shard_map/all_to_all | solution.py:94
  36.5 0.5 broadcast.187
  37.0 0.6 reduce.5
  37.7 6.7 %all-to-all-done.1 = bf16[32,4,128]{2,1,0:T(4,128)(2,1)S(1)} async-done(((bf16[32,4,128]{2,1,0:T(4,128)(2,1)}), bf16[32,4,128]{2,1,0:T(4,128)(2,1)S(1)}, u32[]{:S(2)}, u32[]{:S(2)}) %all-to-all-start.1) | async-done | bytes 32800 | tf_op jit(solution)/shard_map/all_to_all | solution.py:94
  44.4 0.9 fusion.17
  45.4 32.9 %all-reduce.6.cloned.1.call-done = f32[448,128]{1,0:T(8,128)} async-done(((f32[448,128]{1,0:T(8,128)}), f32[448,128]{1,0:T(8,128)}) %all-reduce.6.cloned.1.call-update) | async-done | bytes 229392 | tf_op jit(solution)/shard_map/psum | solution.py:98
  78.3 1.0 broadcast_multiply_fusion
  79.3 1.0 fusion.18
  80.3 0.8 select_n.68
  81.1 36.1 %all-reduce.8.cloned.1.call-done = bf16[448,128]{1,0:T(8,128)(2,1)} async-done(((bf16[448,128]{1,0:T(8,128)(2,1)}), bf16[448,128]{1,0:T(8,128)(2,1)}) %all-reduce.8.cloned.1.call-update) | async-done | bytes 114704 | tf_op jit(solution)/shard_map/psum | solution.py:11
  117.3 0.1 lt.90
  117.9 4.2 %copy.33 = f32[16,16,3584]{2,1,0:T(8,128)} copy(f32[16,16,3584]{2,1,0:T(8,128)} %bitcast.86) | data formatting | bytes 7340032
  122.1 77.2 %all-gather.2.cloned.1.call-done = bf16[14336,128]{1,0:T(8,128)(2,1)} async-done(((bf16[448,128]{1,0:T(8,128)(2,1)}), bf16[14336,128]{1,0:T(8,128)(2,1)}) %all-gather.2.cloned.1.call-update) | async-done | bytes 3670032 | tf_op jit(solution)/shard_map/all_gather | solution.py:108
  199.3 3.2 %gather_fusion.1 = bf16[128,128]{1,0:T(8,128)(2,1)S(1)} fusion(bf16[14336,128]{1,0:T(8,128)(2,1)} %all-gather.2.cloned.1.call-done, s32[1024]{0:T(1024)S(1)} %pad_clamp_fusion), kind=kCustom, calls=%fused_computation.1 | custom fusion | bytes 66048 | tf_op jit(solution)/shard_map/gather | solution.py:110
  202.5 3.5 %fusion = f32[32,4,1,128]{3,2,1,0:T(1,128)S(1)} fusion(bf16[1,1,32,4,128,128]{5,4,3,2,1,0:T(8,128)(2,1)} %param.21, bf16[32,4,128,1]{2,1,0,3:T(4,128)(2,1)S(1)} %bitcast.88), kind=kOutput, calls=%fused_computation.5 | convolution fusion | flops 4194304 | bytes 4292608 | tf_op jit(solution)/shard_map/hgw,hgwy->hgy/dot_general | solution.py:111
  206.0 0.1 broadcast_select_fusion
  206.1 0.2 convolution_multiply_fusion
  206.4 1.7 bitcast_dynamic-update-slice_fusion
  208.1 2.4 fusion.25
  210.4 2.1 collective-permute-start.1
  212.5 8.3 %collective-permute-start = (f32[16,1,3584]{2,1,0:T(1,128)S(1)}, f32[16,1,3584]{2,1,0:T(1,128)S(1)}, u32[]{:S(2)}, u32[]{:S(2)}) collective-permute-start(f32[16,1,3584]{2,1,0:T(1,128)S(1)} %get-tuple-element.22), channel_id=1, source_target_pairs={{1,0},{2,1},{3,2},{4,3},{5,4},{6,5},{7,6},{8,7},{9,8},{10,9},{11,1... | collective-permute-start | bytes 688136 | tf_op jit(solution)/shard_map/ppermute | solution.py:24
  220.9 2.9 %collective-permute-done.1 = f32[16,1,3584]{2,1,0:T(1,128)S(1)} collective-permute-done((f32[16,1,3584]{2,1,0:T(1,128)S(1)}, f32[16,1,3584]{2,1,0:T(1,128)S(1)}, u32[]{:S(2)}, u32[]{:S(2)}) %collective-permute-start.1) | collective-permute-done | bytes 229408 | tf_op jit(solution)/shard_map/ppermute | solution.py:22
  223.8 1.2 collective-permute-done
  225.0 11.7 %fusion.5 = f32[16,16,3584]{2,1,0:T(8,128)S(1)} fusion(f32[16,16,3584]{2,1,0:T(8,128)} %bitcast_dynamic-update-slice_fusion, f32[16,1,3584]{2,1,0:T(1,128)S(1)} %collective-permute-done, f32[16,1,3584]{2,1,0:T(1,128)S(1)} %collective-permute-done.1, bf16[1,16,16,3584]{3,2,1,0:T(8,128)(2,1)S(1)} %copy-done.1, f32[16,3584]{1,0:T(8,128)S(1)} %convert_select_fusion, ...), kind=kLoop, calls=%fused_computation.10 | loop fusion | flops 19267584 | bytes 13533184 | tf_op jit(solution)/shard_map/mul | solution.py:44
  236.7 0.3 fusion.24
  237.0 1.9 collective-permute-start.3
  238.9 8.9 %collective-permute-start.2 = (f32[16,1,3584]{2,1,0:T(1,128)S(1)}, f32[16,1,3584]{2,1,0:T(1,128)S(1)}, u32[]{:S(2)}, u32[]{:S(2)}) collective-permute-start(f32[16,1,3584]{2,1,0:T(1,128)S(1)} %get-tuple-element.20), channel_id=1, source_target_pairs={{1,0},{2,1},{3,2},{4,3},{5,4},{6,5},{7,6},{8,7},{9,8},{10,9},{11,1... | collective-permute-start | bytes 688136 | tf_op jit(solution)/shard_map/ppermute | solution.py:24
  247.8 2.1 collective-permute-done.3
  249.9 1.5 collective-permute-done.2
  251.3 3.9 %fusion.7 = f32[16,16,3584]{2,1,0:T(8,128)S(1)} fusion(f32[16,16,3584]{2,1,0:T(8,128)S(1)} %fusion.5, f32[16,1,3584]{2,1,0:T(1,128)S(1)} %collective-permute-done.2, f32[16,1,3584]{2,1,0:T(1,128)S(1)} %collective-permute-done.3, bf16[1,16,16,3584]{3,2,1,0:T(8,128)(2,1)S(1)} %copy-done.1, f32[16,3584]{1,0:T(8,128)S(1)} %convert_select_fusion, ...), kind=kLoop, calls=%fused_computation.12 | loop fusion | flops 19267584 | bytes 13533184 | tf_op jit(solution)/shard_map/mul | solution.py:44
  255.3 0.3 fusion.23
  255.6 1.9 collective-permute-start.5
  257.5 8.9 %collective-permute-start.4 = (f32[16,1,3584]{2,1,0:T(1,128)S(1)}, f32[16,1,3584]{2,1,0:T(1,128)S(1)}, u32[]{:S(2)}, u32[]{:S(2)}) collective-permute-start(f32[16,1,3584]{2,1,0:T(1,128)S(1)} %get-tuple-element.18), channel_id=1, source_target_pairs={{1,0},{2,1},{3,2},{4,3},{5,4},{6,5},{7,6},{8,7},{9,8},{10,9},{11,1... | collective-permute-start | bytes 688136 | tf_op jit(solution)/shard_map/ppermute | solution.py:24
  266.5 2.1 collective-permute-done.5
  268.5 1.5 collective-permute-done.4
  270.0 5.2 %fusion.10 = f32[1,16,16,3584]{3,2,1,0:T(8,128)} fusion(f32[16,16,3584]{2,1,0:T(8,128)S(1)} %fusion.7, f32[16,1,3584]{2,1,0:T(1,128)S(1)} %collective-permute-done.4, f32[16,1,3584]{2,1,0:T(1,128)S(1)} %collective-permute-done.5, bf16[1,16,16,3584]{3,2,1,0:T(8,128)(2,1)S(1)} %copy-done.1, f32[16,3584]{1,0:T(8,128)S(1)} %convert_select_fusion, ...), kind=kLoop, calls=%fused_computation.15 | loop fusion | flops 19267584 | bytes 13533184 | tf_op jit(solution)/shard_map/broadcast_in_dim | solution.py:138
  (33 shorter events, 1.0 us)
Async XLA Ops:
  6.5 72.7 %copy-start.2 = (s32[16,3584]{1,0:T(8,128)S(1)}, s32[16,3584]{1,0:T(8,128)}, u32[]{:S(2)}) copy-start(s32[16,3584]{1,0:T(8,128)} %param.15) | copy-start | bytes 688132
  8.0 19.0 %all-to-all-start = ((s32[32,1,4]{2,1,0:T(1,128)}), s32[32,1,4]{2,1,0:T(1,128)S(1)}, u32[]{:S(2)}, u32[]{:S(2)}) async-start(s32[32,1,4]{2,1,0:T(1,128)} %copy.19), calls=%async_computation | async-start | bytes 32768 | tf_op jit(solution)/shard_map/all_to_all | solution.py:95
  22.5 94.7 %copy-start.4 = (s32[1,1,32]{2,1,0:T(1,128)S(1)}, s32[1,1,32]{2,1,0:T(1,128)}, u32[]{:S(2)}) copy-start(s32[1,1,32]{2,1,0:T(1,128)} %param.20) | copy-start | bytes 388
  22.5 94.9 %slice-start = ((s32[1,1,2,32,4]{3,4,2,1,0:T(4,128)}), s32[1,1,1,32,4]{3,4,2,1,0:T(4,128)S(1)}, s32[]{:S(2)}) async-start(s32[1,1,2,32,4]{3,4,2,1,0:T(4,128)} %param.19), calls=%async_computation.5 | async-start | bytes 4096 | tf_op jit(solution)/shard_map/slice | solution.py:119
  22.5 95.1 %copy-start.3 = (s32[1,1,2,32,4]{3,4,2,1,0:T(4,128)S(1)}, s32[1,1,2,32,4]{3,4,2,1,0:T(4,128)}, u32[]{:S(2)}) copy-start(s32[1,1,2,32,4]{3,4,2,1,0:T(4,128)} %param.19) | copy-start | bytes 3076
  26.9 17.5 %all-to-all-start.1 = ((bf16[32,4,128]{2,1,0:T(4,128)(2,1)}), bf16[32,4,128]{2,1,0:T(4,128)(2,1)S(1)}, u32[]{:S(2)}, u32[]{:S(2)}) async-start(bf16[32,4,128]{2,1,0:T(4,128)(2,1)} %select_convert_fusion), calls=%async_computation.1 | async-start | bytes 65536 | tf_op jit(solution)/shard_map/all_to_all | solution.py:94
  36.5 41.8 %all-reduce.6.cloned.1.call-start = ((), (), s32[]{:S(2)}) async-start(), calls=%async_computation.2 | async-start | bytes 458752 | tf_op jit(solution)/shard_map/psum | solution.py:98
  45.3 71.9 %all-reduce.8.cloned.1.call-start = ((), (), s32[]{:S(2)}) async-start(), calls=%async_computation.3 | async-start | bytes 229376 | tf_op jit(solution)/shard_map/psum | solution.py:11
  81.1 118.2 %all-gather.2.cloned.1.call-start = ((), (), s32[]{:S(2)}) async-start(), calls=%async_computation.4 | async-start | bytes 3784704 | tf_op jit(solution)/shard_map/all_gather | solution.py:108
  202.5 22.5 %copy-start.1 = (bf16[1,16,16,3584]{3,2,1,0:T(8,128)(2,1)S(1)}, bf16[1,16,16,3584]{3,2,1,0:T(8,128)(2,1)}, u32[]{:S(2)}) copy-start(bf16[1,16,16,3584]{3,2,1,0:T(8,128)(2,1)} %param.14) | copy-start | bytes 5505028
  210.4 13.3 %collective-permute-start.1 = (f32[16,1,3584]{2,1,0:T(1,128)S(1)}, f32[16,1,3584]{2,1,0:T(1,128)S(1)}, u32[]{:S(2)}, u32[]{:S(2)}) collective-permute-start(f32[16,1,3584]{2,1,0:T(1,128)S(1)} %get-tuple-element.21), channel_id=1, source_target_pairs={{0,1},{1,2},{2,3},{3,4},{4,5},{5,6},{6,7},{7,8},{8,9},{9,10},{10,1... | collective-permute-start | bytes 688136 | tf_op jit(solution)/shard_map/ppermute | solution.py:22
  212.5 12.4 %collective-permute-start = (f32[16,1,3584]{2,1,0:T(1,128)S(1)}, f32[16,1,3584]{2,1,0:T(1,128)S(1)}, u32[]{:S(2)}, u32[]{:S(2)}) collective-permute-start(f32[16,1,3584]{2,1,0:T(1,128)S(1)} %get-tuple-element.22), channel_id=1, source_target_pairs={{1,0},{2,1},{3,2},{4,3},{5,4},{6,5},{7,6},{8,7},{9,8},{10,9},{11,1... | collective-permute-start | bytes 688136 | tf_op jit(solution)/shard_map/ppermute | solution.py:24
  220.8 30.5 %copy-start = (bf16[2,1,16,16,3584]{4,3,2,1,0:T(8,128)(2,1)S(1)}, bf16[2,1,16,16,3584]{4,3,2,1,0:T(8,128)(2,1)}, u32[]{:S(2)}) copy-start(bf16[2,1,16,16,3584]{4,3,2,1,0:T(8,128)(2,1)} %param.13) | copy-start | bytes 11010052
  237.0 12.9 %collective-permute-start.3 = (f32[16,1,3584]{2,1,0:T(1,128)S(1)}, f32[16,1,3584]{2,1,0:T(1,128)S(1)}, u32[]{:S(2)}, u32[]{:S(2)}) collective-permute-start(f32[16,1,3584]{2,1,0:T(1,128)S(1)} %get-tuple-element.19), channel_id=1, source_target_pairs={{0,1},{1,2},{2,3},{3,4},{4,5},{5,6},{6,7},{7,8},{8,9},{9,10},{10,1... | collective-permute-start | bytes 688136 | tf_op jit(solution)/shard_map/ppermute | solution.py:22
  238.9 12.4 %collective-permute-start.2 = (f32[16,1,3584]{2,1,0:T(1,128)S(1)}, f32[16,1,3584]{2,1,0:T(1,128)S(1)}, u32[]{:S(2)}, u32[]{:S(2)}) collective-permute-start(f32[16,1,3584]{2,1,0:T(1,128)S(1)} %get-tuple-element.20), channel_id=1, source_target_pairs={{1,0},{2,1},{3,2},{4,3},{5,4},{6,5},{7,6},{8,7},{9,8},{10,9},{11,1... | collective-permute-start | bytes 688136 | tf_op jit(solution)/shard_map/ppermute | solution.py:24
  255.6 12.9 %collective-permute-start.5 = (f32[16,1,3584]{2,1,0:T(1,128)S(1)}, f32[16,1,3584]{2,1,0:T(1,128)S(1)}, u32[]{:S(2)}, u32[]{:S(2)}) collective-permute-start(f32[16,1,3584]{2,1,0:T(1,128)S(1)} %get-tuple-element.17), channel_id=1, source_target_pairs={{0,1},{1,2},{2,3},{3,4},{4,5},{5,6},{6,7},{7,8},{8,9},{9,10},{10,1... | collective-permute-start | bytes 688136 | tf_op jit(solution)/shard_map/ppermute | solution.py:22
  257.5 12.4 %collective-permute-start.4 = (f32[16,1,3584]{2,1,0:T(1,128)S(1)}, f32[16,1,3584]{2,1,0:T(1,128)S(1)}, u32[]{:S(2)}, u32[]{:S(2)}) collective-permute-start(f32[16,1,3584]{2,1,0:T(1,128)S(1)} %get-tuple-element.18), channel_id=1, source_target_pairs={{1,0},{2,1},{3,2},{4,3},{5,4},{6,5},{7,6},{8,7},{9,8},{10,9},{11,1... | collective-permute-start | bytes 688136 | tf_op jit(solution)/shard_map/ppermute | solution.py:24
Sparse Core Ops, SparseCore 0:
  45.5 32.7 all-reduce.5
  81.2 35.9 all-reduce.7
  120.3 78.9 all-gather.1
where the time goes:
time: 283 us; the launch traced here: 282 us
  waiting for transfers between devices  164 us (58%)
  starting transfers between devices  52.7 us (19%)
  other arithmetic  28.1 us (10%)
  local copies, waits for them, and re-layouts  15.1 us (5%)
  between operations  13.4 us (5%)
  matrix products  8 us (3%)
    all_gather x1, waiting for transfers between devices, per_device(): lax.all_gather(shard_heat_field, 'tile', axis=0, tiled=True)  77.2 us
    psum x1, waiting for transfers between devices, from_root(): return lax.psum(block, axis)  36.1 us
    psum x1, waiting for transfers between devices, per_device(): ocean_flux = lax.psum(partial_value, 'sect')  32.9 us
    ppermute x3, starting transfers between devices, with_halo(): lax.ppermute(head, axis, [((i + 1) % count, i) for i in range(ends)])  26.1 us
    mul x2, other arithmetic, stencil(): return updated * wet_mask  15.6 us
    all_to_all x1, starting transfers between devices, per_device(): lax.all_to_all(target_ids, 'tile', split_axis=0, concat_axis=0, tiled=True)  11.1 us
    all_to_all x1, starting transfers between devices, per_device(): lax.all_to_all(products, 'tile', split_axis=0, concat_axis=0, tiled=True)  9.52 us
    ppermute x3, waiting for transfers between devices, with_halo(): lax.ppermute(tail, axis, [(i, (i + 1) % count) for i in range(ends)])  7.05 us
  transfers between devices with their start and end apart: 11, of which 11 were waited for; matrix products, arithmetic and copies ran while one was open for 5% of the time, Pallas kernels for 0%

commit v1 on v0

v1 whole, which is shorter than its diff:
```python
import functools

import jax
import jax.numpy as jnp
from jax import lax
from jax.experimental import pallas as pl
from jax.experimental.pallas import tpu as pltpu
from jax.sharding import PartitionSpec as P

F32 = jnp.float32
BF16 = jnp.bfloat16
MESH = pl.DeviceIdType.MESH
LANES = 128
SUBSTEPS = 3
CODE = 1024


def shifted_rows(upper, lower, north, south):
    row = lax.broadcasted_iota(jnp.int32, upper.shape, 0)
    upper_down = pltpu.roll(upper, 1, 0)
    lower_down = pltpu.roll(lower, 1, 0)
    upper_up = pltpu.roll(upper, 7, 0)
    lower_up = pltpu.roll(lower, 7, 0)
    return (
        jnp.where(row == 0, north, upper_down),
        jnp.where(row == 0, upper_down, lower_down),
        jnp.where(row == 7, lower_up, upper_up),
        jnp.where(row == 7, south, lower_up),
    )


def column_chunks(width, tiles):
    step = tiles * LANES
    return [(start, step) for start in range(0, width, step)]


def shifted_columns(x, before, after):
    size = x.shape[1]
    lane = lax.broadcasted_iota(jnp.int32, before.shape, 1)
    east = pltpu.roll(x, size - 1, 1)
    west = pltpu.roll(x, 1, 1)
    east_end = jnp.where(lane == LANES - 1, pltpu.roll(after, LANES - 1, 1), east[:, size - LANES :])
    west_end = jnp.where(lane == 0, pltpu.roll(before, 1, 1), west[:, :LANES])
    return (
        jnp.concatenate([east[:, : size - LANES], east_end], axis=1),
        jnp.concatenate([west_end, west[:, LANES:]], axis=1),
    )


def substep_level(src, dst, coef, halo_rows, level, keep):
    columns = src.shape[-1]
    north = halo_rows[0, pl.ds(level, 1), :]
    south = halo_rows[1, pl.ds(level, 1), :]
    for start, size in column_chunks(columns, 7):
        cols = pl.ds(start, size)
        upper = src[level, 0:8, cols]
        lower = src[level, 8:16, cols]
        upper_n, lower_n, upper_s, lower_s = shifted_rows(
            upper, lower, north[:, start : start + size], south[:, start : start + size]
        )
        before = pl.ds((start - LANES) % columns, LANES)
        after = pl.ds((start + size) % columns, LANES)
        results = []
        for x, xn, xs, row in ((upper, upper_n, upper_s, 0), (lower, lower_n, lower_s, 8)):
            rows = pl.ds(row, 8)
            east, west = shifted_columns(x, src[level, rows, before], src[level, rows, after])
            new = (
                coef[0, level, rows, cols] * x
                + coef[1, level, rows, cols] * east
                + coef[2, level, rows, cols] * west
                + coef[3, level, rows, cols] * xn
                + coef[4, level, rows, cols] * xs
            )
            dst[level, rows, cols] = new
            results.append(new)
        if keep is not None:
            keep(results[0], results[1], start, size)


def over_levels(first, count, act, unroll=4):
    def some(i, carry):
        for j in range(unroll):
            act(first + i * unroll + j)
        return carry

    lax.fori_loop(0, count // unroll, some, 0)
    for level in range(first + count // unroll * unroll, first + count):
        act(level)


def coefficients(u, v, k, wet, first, last):
    u = 0.5 * u
    v = 0.5 * v
    east = k - u
    west = k + u
    col = lax.broadcasted_iota(jnp.int32, u.shape, 1)
    if first is not None:
        west = jnp.where(col == first, 0.0, west)
    if last is not None:
        east = jnp.where(col == last, 0.0, east)
    parts = (1.0 - 4.0 * k, east, west, k + v, k - v)
    return parts if wet is None else [wet * c for c in parts]


def kernel_body(
    sections,
    tiles,
    tracer,
    courant,
    diffusion,
    water,
    down_pairs,
    down_number,
    down_matrix,
    up_pairs,
    up_number,
    up_matrix,
    field_b,
    field_a,
    winds,
    mixing,
    coef,
    mask_int,
    wet_mask,
    pairs_d,
    number_d,
    matrix_d,
    pairs_u,
    number_u,
    matrix_u,
    down_send,
    down_recv,
    up_send,
    up_recv,
    lhs_all,
    onehot_up,
    sst,
    halo_stage,
    halo_rows,
    halo_send,
    halo_recv,
    scale_send,
    scale_recv,
    edge_send,
    edge_recv,
    side_send,
    side_recv,
    zero_a,
    zero_b,
    coef_zero,
    load_sem,
    remap_sem,
    halo_sems,
    scale_sems,
    edge_sems,
    side_sems,
):
    sect = lax.axis_index("sect")
    tile = lax.axis_index("tile")
    ocean_sect = sections - 1
    is_ocean = sect == ocean_sect
    is_atm = sect != ocean_sect
    has_north = tile > 0
    has_south = tile < tiles - 1
    levels, rows, columns = field_a.shape
    col_tiles = columns // LANES
    blocks = rows * col_tiles
    blocks_pad = 512
    lanes_i = functools.partial(lax.broadcasted_iota, jnp.int32)

    def load(src, dst, number):
        return pltpu.make_async_copy(src, dst, load_sem.at[number])

    loads = [
        load(tracer.at[pl.ds(0, 1)], field_a.at[pl.ds(0, 1)], 0),
        load(down_pairs, pairs_d, 1),
        load(down_number, number_d, 2),
        load(up_pairs, pairs_u, 3),
        load(up_number, number_u, 4),
        load(down_matrix, matrix_d, 5),
        load(tracer.at[pl.ds(1, levels - 1)], field_a.at[pl.ds(1, levels - 1)], 6),
        load(water, mask_int, 7),
        load(courant, winds, 8),
        load(diffusion, mixing, 9),
        load(up_matrix, matrix_u, 10),
    ]
    for copy in loads:
        copy.start()

    barrier = pltpu.get_barrier_semaphore()

    def greet(device):
        pl.semaphore_signal(barrier, inc=1, device_id=device, device_id_type=MESH)

    @pl.when(is_atm)
    def _():
        def one(i, carry):
            greet((ocean_sect, lax.rem(tile + i, tiles)))
            return carry

        lax.fori_loop(0, tiles, one, 0)

    @pl.when(is_ocean)
    def _():
        def one(i, carry):
            for s in range(ocean_sect):
                greet((s, lax.rem(tile + i, tiles)))
            return carry

        lax.fori_loop(0, tiles, one, 0)

    @pl.when(has_north)
    def _():
        greet((sect, tile - 1))

    @pl.when(has_south)
    def _():
        greet((sect, tile + 1))

    for edge, number in ((has_north, 0), (has_south, 1)):

        @pl.when(jnp.logical_not(edge))
        def _(number=number):
            for step in range(SUBSTEPS):
                halo_recv[step, number] = jnp.zeros(halo_recv.shape[2:], halo_recv.dtype)
                scale_recv[step, number] = jnp.zeros(scale_recv.shape[2:], F32)
            edge_recv[number] = jnp.zeros(edge_recv.shape[1:], F32)
            side_recv[number] = jnp.zeros(side_recv.shape[1:], BF16)

    for number in (1, 2, 3, 4):
        loads[number].wait()

    slots = pairs_d.shape[1]
    eye = lanes_i((tiles, tiles), 0) == lanes_i((tiles, tiles), 1)

    def ids_by_tile(pairs_ref, number_ref, which, targets):
        ids = pairs_ref[which].astype(F32)
        if targets:
            live = lanes_i((slots, tiles), 0) < number_ref[...]
            ids = jnp.where(live, ids + 1.0, 0.0)
        return [jnp.sum(jnp.where(eye, ids[c : c + 1], 0.0), axis=1, keepdims=True) for c in range(slots)]

    down_src = [ids + 1.0 for ids in ids_by_tile(pairs_d, number_d, 0, False)]
    down_dst = ids_by_tile(pairs_d, number_d, 1, True)
    up_src = ids_by_tile(pairs_u, number_u, 0, False)
    up_dst = ids_by_tile(pairs_u, number_u, 1, True)
    lane = lanes_i((tiles, LANES), 1)

    def block_of(index):
        return (index % rows) * col_tiles + index // rows

    place = lax.rem(tile, 16) * 8
    target_row = jnp.zeros((tiles, LANES), F32)
    for c in range(slots):
        target_row = jnp.where(lane == place + c, down_dst[c], target_row)
    for c in range(slots):
        ids = jnp.broadcast_to(up_src[c], (tiles, LANES))
        if c == 0:
            ids = ids + CODE * target_row
        down_send[:, 4 + c, :] = ids

    def row_of_ids(ids, first, count):
        dest = lanes_i((count, 8 * count), 0)
        at = lanes_i((count, 8 * count), 1)
        spread = jnp.zeros((count, 8 * count), F32)
        for c in range(slots):
            spread = jnp.where(at == 8 * dest + c, ids[c][first : first + count], spread)
        return jnp.sum(spread, axis=0, keepdims=True)

    @pl.when(is_atm)
    def _():
        place_block = (block_of(lanes_i((blocks, LANES), 0)) + 1).astype(F32)
        for half in range(tiles // 16):
            ids = pltpu.roll(row_of_ids(up_dst, 16 * half, 16), 4, 1)
            onehot_up[:, half * LANES : (half + 1) * LANES] = jnp.where(place_block == ids, 1.0, 0.0).astype(BF16)

    loads[0].wait()

    @pl.when(is_atm)
    def _():
        for k in range(col_tiles):
            sst[k * rows : (k + 1) * rows, :] = field_a[0, :, k * LANES : (k + 1) * LANES].astype(BF16)
        sst[blocks:blocks_pad, :] = jnp.zeros((blocks_pad - blocks, LANES), BF16)
        place_block = (block_of(lanes_i((blocks_pad, LANES), 0)) + 1).astype(F32)
        for half in range(tiles // 16):
            ids = row_of_ids(down_src, 16 * half, 16)
            onehot = jnp.where(place_block == ids, 1.0, 0.0).astype(BF16)
            picked = lax.dot_general(onehot, sst[...], (((0,), (0,)), ((), ())), preferred_element_type=F32)
            lhs_all[half * 16 : (half + 1) * 16] = picked.reshape(16, 8, LANES)

    def remap(rows_ref, matrix_ref, first, tile_index):
        x = rows_ref[tile_index]
        sub = lanes_i((8, LANES), 0)
        lhs = jnp.concatenate([jnp.where(sub == first + c, x, 0.0) for c in range(slots)], axis=1).astype(BF16)
        matrix = matrix_ref[tile_index].reshape(slots * LANES, LANES)
        return jnp.dot(lhs, matrix, preferred_element_type=F32)

    loads[5].wait()

    @pl.when(is_atm)
    def _():
        def some(i, carry):
            for j in range(8):
                d = i * 8 + j
                product = remap(lhs_all, matrix_d, 0, d).astype(BF16).astype(F32)
                down_send[d, 0:4, :] = product[0:4]
            return carry

        lax.fori_loop(0, tiles // 8, some, 0)

    pl.semaphore_wait(
        barrier,
        jnp.where(is_atm, tiles, ocean_sect * tiles) + has_north.astype(jnp.int32) + has_south.astype(jnp.int32),
    )

    @pl.when(is_atm)
    def _():
        def one(i, carry):
            d = lax.rem(tile + i, tiles)
            pltpu.make_async_remote_copy(
                src_ref=down_send.at[d],
                dst_ref=down_recv.at[sect * tiles + tile],
                send_sem=remap_sem.at[0],
                recv_sem=remap_sem.at[1],
                device_id=(ocean_sect, d),
                device_id_type=MESH,
            ).start()
            return carry

        lax.fori_loop(0, tiles, one, 0)

    def neighbour_copy(send, recv, sems, number):
        to = (sect, tile + 1) if number == 0 else (sect, tile - 1)
        return pltpu.make_async_remote_copy(
            src_ref=send,
            dst_ref=recv,
            send_sem=sems.at[0],
            recv_sem=sems.at[1],
            device_id=to,
            device_id_type=MESH,
        )

    def for_each_side(act):
        for number, sends, receives in ((0, has_south, has_north), (1, has_north, has_south)):
            act(number, sends, receives)

    def exchange(make):
        def act(number, sends, receives):
            @pl.when(sends)
            def _():
                make(number).start()

        for_each_side(act)

    def settle(make, sent, received):
        def act(number, sends, receives):
            if sent:

                @pl.when(sends)
                def _():
                    make(number).wait_send()

            if received:

                @pl.when(receives)
                def _():
                    make(number).wait_recv()

        for_each_side(act)

    def halo(step, group):
        def make(number):
            return neighbour_copy(
                halo_send.at[step, number, group],
                halo_recv.at[step, number, group],
                halo_sems.at[step, group, number],
                number,
            )

        return make

    def scale(step, group):
        def make(number):
            return neighbour_copy(
                scale_send.at[step, number, group],
                scale_recv.at[step, number, group],
                scale_sems.at[step, group, number],
                number,
            )

        return make

    half = columns // 2
    quarter = columns // 4

    def send_halo(step, group):
        part = pl.ds(8 * group, 8)
        for number in range(2):
            chunks = [halo_stage[number, part, pl.ds(q * quarter, quarter)] for q in range(4)]
            most = functools.reduce(jnp.maximum, [jnp.abs(chunk) for chunk in chunks])
            most = functools.reduce(
                jnp.maximum, [most[:, k * LANES : (k + 1) * LANES] for k in range(quarter // LANES)]
            )
            most = jnp.maximum(most, 1e-33)
            scale_send[step, number, group] = most * (1.0 / 32767.0)
            factor = jnp.concatenate([32767.0 / most] * (quarter // LANES), axis=1)
            for q in range(2):
                both = jnp.concatenate([chunks[q] * factor, chunks[q + 2] * factor], axis=0)
                halo_send[step, number, group, :, pl.ds(q * quarter, quarter)] = (
                    jnp.round(both).astype(jnp.int32).astype(jnp.int16)
                )
        exchange(scale(step, group))
        exchange(halo(step, group))

    def take_halo(step, group):
        settle(scale(step, group), False, True)
        settle(halo(step, group), False, True)
        part = pl.ds(8 * group, 8)
        for number in range(2):
            factor = jnp.concatenate([scale_recv[step, number, group]] * (quarter // LANES), axis=1)
            for q in range(2):
                both = halo_recv[step, number, group, :, pl.ds(q * quarter, quarter)].astype(jnp.int32).astype(F32)
                halo_rows[number, part, pl.ds(q * quarter, quarter)] = both[0:8] * factor
                halo_rows[number, part, pl.ds(half + q * quarter, quarter)] = both[8:16] * factor

    def edge(number):
        return neighbour_copy(edge_send.at[number], edge_recv.at[number], edge_sems.at[number], number)

    def side(number):
        return neighbour_copy(side_send.at[number], side_recv.at[number], side_sems.at[number], number)

    loads[6].wait()

    group_levels = ((1, 7), (8, 8))
    halo_stage[:, 0:1, :] = jnp.zeros((2, 1, columns), F32)
    for group in range(2):

        def rows_out(level):
            halo_stage[0, pl.ds(level, 1), :] = field_a[level, 15:16, :]
            halo_stage[1, pl.ds(level, 1), :] = field_a[level, 0:1, :]

        over_levels(*group_levels[group], rows_out)
        send_halo(0, group)

    loads[7].wait()
    loads[8].wait()
    loads[9].wait()
    wet_mask[...] = jnp.where(is_ocean, mask_int[...].astype(F32), 1.0)

    for number, row in ((0, 14), (1, 0)):
        pair = slice(row, row + 2)
        packed = jnp.concatenate(
            [
                winds[0, 0][pair].astype(F32),
                winds[1, 0][pair].astype(F32),
                mixing[0][pair].astype(F32),
                wet_mask[row : row + 2, :],
            ],
            axis=0,
        )
        side_send[number] = jnp.concatenate([packed[:, :half], packed[:, half:]], axis=0).astype(BF16)
    exchange(side)

    def coef_level(wet_ref, level):
        for start, size in column_chunks(columns, 7):
            cols = pl.ds(start, size)
            parts = coefficients(
                winds[0, level, :, cols].astype(F32),
                winds[1, level, :, cols].astype(F32),
                mixing[level, :, cols].astype(F32),
                None if wet_ref is None else wet_ref[:, cols],
                0 if start == 0 else None,
                size - 1 if start + size == columns else None,
            )
            for i, part in enumerate(parts):
                coef[i, level, :, cols] = part

    for here, wet_ref in ((is_atm, None), (is_ocean, wet_mask)):

        @pl.when(here)
        def _(wet_ref=wet_ref):
            over_levels(0, levels, functools.partial(coef_level, wet_ref), 2)

    @pl.when(is_ocean)
    def _():
        pltpu.make_async_copy(down_recv, down_recv, remap_sem.at[1]).wait()
        count = ocean_sect * tiles * 8
        arrived = down_recv[...]
        codes = arrived.astype(jnp.int32)
        targets = codes >> 10
        sources = codes & (CODE - 1)
        place_block = block_of(lanes_i((blocks, LANES), 0)) + 1
        onehots = []
        for q in range(count // LANES):
            ids = jnp.sum(targets[q * 16 : (q + 1) * 16, 4:5, :], axis=0)
            onehots.append(jnp.where(place_block == ids, 1.0, 0.0).astype(BF16))
        flux = jnp.dot(
            jnp.concatenate(onehots, axis=1),
            arrived.reshape(count, LANES).astype(BF16),
            preferred_element_type=F32,
        )
        for k in range(col_tiles):
            cols = pl.ds(k * LANES, LANES)
            wet = wet_mask[:, cols]
            warm = field_a[0, :, cols] + flux[k * rows : (k + 1) * rows] * wet
            zero_a[8:24, cols] = warm
            sst[k * rows : (k + 1) * rows, :] = (warm * wet).astype(BF16)
        sst[blocks:blocks_pad, :] = jnp.zeros((blocks_pad - blocks, LANES), BF16)
        asked = sources.reshape(count, LANES)
        gathers = [
            jnp.where(asked == block_of(lanes_i((count, LANES), 1) + q * LANES), 1.0, 0.0).astype(BF16)
            for q in range(blocks_pad // LANES)
        ]
        up_send[...] = jnp.dot(jnp.concatenate(gathers, axis=1), sst[...], preferred_element_type=F32).reshape(
            up_send.shape
        )

        def one(i, carry):
            t = lax.rem(tile + i, tiles)
            for s in range(ocean_sect):
                pltpu.make_async_remote_copy(
                    src_ref=up_send.at[s * tiles + t],
                    dst_ref=up_recv.at[tile],
                    send_sem=remap_sem.at[2],
                    recv_sem=remap_sem.at[3],
                    device_id=(s, t),
                    device_id_type=MESH,
                ).start()
            return carry

        lax.fori_loop(0, tiles, one, 0)

    def send_edges():
        for start, size in column_chunks(columns, 7):
            cols = pl.ds(start, size)
            edge_send[0, :, cols] = zero_a[20:24, cols]
            edge_send[1, :, cols] = zero_a[8:12, cols]
        exchange(edge)

    @pl.when(is_ocean)
    def _():
        send_edges()

    fields = (field_a, field_b, field_a, field_b)

    def run_group(step, group):
        src, dst = fields[step], fields[step + 1]
        take_halo(step, group)
        last = step == SUBSTEPS - 1

        def keep_rows(level):
            def keep(upper, lower, start, size):
                cols = pl.ds(start, size)
                halo_stage[0, pl.ds(level, 1), cols] = lower[7:8]
                halo_stage[1, pl.ds(level, 1), cols] = upper[0:1]

            return keep

        def one(level):
            substep_level(src, dst, coef, halo_rows, level, None if last else keep_rows(level))

        over_levels(*group_levels[group], one)
        if not last:
            send_halo(step + 1, group)

    run_group(0, 0)
    run_group(0, 1)

    loads[10].wait()

    @pl.when(is_atm)
    def _():
        pltpu.make_async_copy(up_recv, up_recv, remap_sem.at[3]).wait()

        def some(i, carry):
            for j in range(8):
                d = i * 8 + j
                lhs_all[d] = remap(up_recv, matrix_u, 4, d)
            return carry

        lax.fori_loop(0, tiles // 8, some, 0)
        returned = lhs_all[...].reshape(8 * tiles, LANES)
        high = returned.astype(BF16)
        rest = returned - high.astype(F32)
        middle = rest.astype(BF16)
        low = (rest - middle.astype(F32)).astype(BF16)
        onehot = onehot_up[...]
        total = jnp.dot(onehot, high, preferred_element_type=F32)
        total = total + jnp.dot(onehot, middle, preferred_element_type=F32)
        total = total + jnp.dot(onehot, low, preferred_element_type=F32)
        for k in range(col_tiles):
            cols = pl.ds(k * LANES, LANES)
            zero_a[8:24, cols] = field_a[0, :, cols] + 0.5 * total[k * rows : (k + 1) * rows]
        send_edges()

    run_group(1, 0)
    run_group(1, 1)

    settle(side, False, True)
    for start, size in column_chunks(columns, 7):
        cols = pl.ds(start, size)
        row = lanes_i((8, size), 0)
        for number, base, shifts, valid in ((0, 0, (6, 4, 2, 0), row >= 6), (1, 24, (0, 6, 4, 2), row < 2)):
            fold = pl.ds(start % half, size)
            packed = side_recv[number, :, fold].astype(F32)[8 * (start // half) : 8 * (start // half) + 8]
            u, v, k, wet = [pltpu.roll(packed, shift, 0) if shift else packed for shift in shifts]
            parts = coefficients(
                u,
                v,
                k,
                wet,
                0 if start == 0 else None,
                size - 1 if start + size == columns else None,
            )
            for i, part in enumerate(parts):
                coef_zero[i, base : base + 8, cols] = jnp.where(valid, part, 0.0)
    settle(edge, False, True)
    for start, size in column_chunks(columns, 7):
        cols = pl.ds(start, size)
        blank = jnp.zeros((4, size), F32)
        zero_a[0:8, cols] = jnp.concatenate([blank, edge_recv[0, :, cols]], axis=0)
        zero_a[24:32, cols] = jnp.concatenate([edge_recv[1, :, cols], blank], axis=0)

    def surface(src, dst, first, count):
        for start, size in column_chunks(columns, 7):
            cols = pl.ds(start, size)
            row = lanes_i((8, size), 0)
            before = pl.ds((start - LANES) % columns, LANES)
            after = pl.ds((start + size) % columns, LANES)
            for g in range(first, first + count):
                here = pl.ds(8 * g, 8)
                x = src[here, cols]
                down = pltpu.roll(x, 1, 0)
                up = pltpu.roll(x, 7, 0)
                if g > 0:
                    down = jnp.where(row == 0, pltpu.roll(src[8 * g - 8 : 8 * g, cols], 1, 0), down)
                if g < 3:
                    up = jnp.where(row == 7, pltpu.roll(src[8 * g + 8 : 8 * g + 16, cols], 7, 0), up)
                east, west = shifted_columns(x, src[here, before], src[here, after])
                if g in (1, 2):
                    inner = pl.ds(8 * g - 8, 8)
                    c = [coef[i, 0, inner, cols] for i in range(5)]
                else:
                    c = [coef_zero[i, here, cols] for i in range(5)]
                new = c[0] * x + c[1] * east + c[2] * west + c[3] * down + c[4] * up
                if dst is None:
                    field_b[0, inner, cols] = new
                else:
                    dst[here, cols] = new

    surface(zero_a, zero_b, 0, 4)
    surface(zero_b, zero_a, 0, 4)
    surface(zero_a, None, 1, 2)

    run_group(2, 0)
    run_group(2, 1)

    @pl.when(is_atm)
    def _():
        pltpu.make_async_copy(down_send, down_send, remap_sem.at[0]).wait()

    @pl.when(is_ocean)
    def _():
        pltpu.make_async_copy(up_send, up_send, remap_sem.at[2]).wait()

    for step in range(SUBSTEPS):
        for group in range(2):
            settle(scale(step, group), True, False)
            settle(halo(step, group), True, False)
    settle(edge, True, False)
    settle(side, True, False)


def write_out(result, out, sem):
    copy = pltpu.make_async_copy(result, out, sem)
    copy.start()
    copy.wait()


def per_device(
    sections,
    tracer_values,
    courant_numbers,
    diffusion_numbers,
    water_indicator,
    downward_lane_pairs,
    downward_lane_number,
    downward_patch_matrix,
    upward_lane_pairs,
    upward_lane_number,
    upward_patch_matrix,
):
    tracer = tracer_values[0]
    levels, rows, columns = tracer.shape
    tiles, slots = downward_lane_pairs.shape[-2:]
    stacked = (SUBSTEPS, 2, levels // 8)
    partners = (sections - 1) * tiles
    blocks = rows * columns // LANES
    vmem = pltpu.VMEM
    dma = pltpu.SemaphoreType.DMA
    whole = pl.BlockSpec(memory_space=pl.ANY)
    operands = (
        tracer,
        courant_numbers[:, 0],
        diffusion_numbers[0],
        water_indicator,
        jnp.swapaxes(downward_lane_pairs[0, 0], 1, 2),
        downward_lane_number[0],
        downward_patch_matrix[0, 0],
        jnp.swapaxes(upward_lane_pairs[0, 0], 1, 2),
        upward_lane_number[0],
        upward_patch_matrix[0, 0],
    )
    result = pl.pallas_call(
        functools.partial(kernel_body, sections, tiles),
        out_shape=pltpu.VMEM(tracer.shape, F32),
        in_specs=[whole] * len(operands),
        out_specs=pl.BlockSpec(memory_space=pltpu.VMEM),
        scratch_shapes=[
            vmem((levels, rows, columns), F32),
            vmem((2, levels, rows, columns), BF16),
            vmem((levels, rows, columns), BF16),
            vmem((5, levels, rows, columns), F32),
            vmem((rows, columns), jnp.int32),
            vmem((rows, columns), F32),
            vmem((2, slots, tiles), jnp.int32),
            vmem((1, tiles), jnp.int32),
            vmem((tiles, slots, LANES, LANES), BF16),
            vmem((2, slots, tiles), jnp.int32),
            vmem((1, tiles), jnp.int32),
            vmem((tiles, slots, LANES, LANES), BF16),
            vmem((tiles, 8, LANES), F32),
            vmem((partners, 8, LANES), F32),
            vmem((partners, 8, LANES), F32),
            vmem((tiles, 8, LANES), F32),
            vmem((tiles, 8, LANES), F32),
            vmem((blocks, 8 * tiles), BF16),
            vmem((512, LANES), BF16),
            vmem((2, levels, columns), F32),
            vmem((2, levels, columns), F32),
            vmem((*stacked, 16, columns // 2), jnp.int16),
            vmem((*stacked, 16, columns // 2), jnp.int16),
            vmem((*stacked, 8, LANES), F32),
            vmem((*stacked, 8, LANES), F32),
            vmem((2, 4, columns), F32),
            vmem((2, 4, columns), F32),
            vmem((2, 16, columns // 2), BF16),
            vmem((2, 16, columns // 2), BF16),
            vmem((32, columns), F32),
            vmem((32, columns), F32),
            vmem((5, 32, columns), F32),
            dma((11,)),
            dma((4,)),
            dma((SUBSTEPS, 2, 2, 2)),
            dma((SUBSTEPS, 2, 2, 2)),
            dma((2, 2)),
            dma((2, 2)),
        ],
        compiler_params=pltpu.CompilerParams(
            collective_id=0, has_side_effects=True, vmem_limit_bytes=54 * 2**20
        ),
    )(*operands)
    result = pl.pallas_call(
        write_out,
        out_shape=jax.ShapeDtypeStruct(tracer.shape, F32),
        in_specs=[pl.BlockSpec(memory_space=pltpu.VMEM)],
        out_specs=whole,
        scratch_shapes=[dma(())],
        compiler_params=pltpu.CompilerParams(vmem_limit_bytes=2**20),
    )(result)
    return result[None]


def solution(mesh):
    placed = (
        P("sect", None, "tile", None),
        P(None, "sect", None, "tile", None),
        P("sect", None, "tile", None),
        P("tile", None),
        P("sect", "tile", None, None, None),
        P("sect", "tile", None),
        P("sect", "tile", None, None, None, None),
        P("sect", "tile", None, None, None),
        P("sect", "tile", None),
        P("sect", "tile", None, None, None, None),
    )
    return jax.shard_map(
        functools.partial(per_device, mesh.shape["sect"]),
        mesh=mesh,
        in_specs=placed,
        out_specs=P("sect", None, "tile", None),
        check_vma=False,
    )
```

time: 283 us -> 37.7 us (0.13)
  waiting for transfers between devices: 164 us -> 0 us
  starting transfers between devices: 52.7 us -> 0 us
  Pallas kernels: 0 us -> 37.6 us
  other arithmetic: 28.1 us -> 0 us
  local copies, waits for them, and re-layouts: 15.1 us -> 0 us
  between operations: 13.4 us -> 0.01 us
  matrix products: 8 us -> 0 us
    all_gather x1 -> x0, waiting for transfers between devices: 77.2 us -> none  [per_device(): lax.all_gather(shard_heat_field, 'tile', axis=0, tiled=True)]
    psum x2 -> x0, waiting for transfers between devices: 68.9 us -> none  [the longest x1 36.1 us: from_root(): return lax.psum(block, axis)]
    pallas_call x0 -> x2, Pallas kernels: none -> 37.6 us  [the longest x1 35.8 us: per_device(): pl.pallas_call(functools.partial(kernel_body, sections, tiles), out_shape...]
    ppermute x6 -> x0, starting transfers between devices: 32 us -> none  [the longest x3 26.1 us: with_halo(): lax.ppermute(head, axis, [((i + 1) % count, i) for i in range(ends)])]
    all_to_all x2 -> x0, starting transfers between devices: 20.6 us -> none  [the longest x1 11.1 us: per_device(): lax.all_to_all(target_ids, 'tile', split_axis=0, concat_axis=0, tiled=True)]
    mul x4 -> x0, other arithmetic: 16.6 us -> none  [the longest x2 15.6 us: stencil(): return updated * wet_mask]
    ppermute x6 -> x0, waiting for transfers between devices: 11.1 us -> none  [the longest x3 7.05 us: with_halo(): lax.ppermute(tail, axis, [(i, (i + 1) % count) for i in range(ends)])]
    dot_general x4 -> x0, matrix products: 8 us -> none  [the longest x1 3.5 us: per_device(): jnp.einsum('hgw,hgwy->hgy', collected_patches, upward_patch_matrix[0, 0],...]
  transfers between devices with their start and end apart: 11 -> 0, of which waited for: 11 -> 0; matrix products, arithmetic and copies ran while one was open for 5% -> 0% of each run, Pallas kernels for 0% -> 0%
where the time goes in v1:
time: 37.7 us; the launch traced here: 37.6 us
  Pallas kernels  37.6 us (100%)
    pallas_call x1, Pallas kernels, per_device(): pl.pallas_call(functools.partial(kernel_body, sections, tiles), out_shape...  35.8 us
    pallas_call x1, Pallas kernels, per_device(): pl.pallas_call(write_out, out_shape=jax.ShapeDtypeStruct(tracer.shape, F3...  1.85 us

profile of v1, /device:TPU:6, one launch (start us, length us, event | category | flops | bytes accessed | tf_op | source)
XLA Modules:
  0.0 37.6 jit_solution(7717742852735838947)
XLA Ops:
  0.0 35.8 %shard_map.100.result = f32[16,16,3584]{2,1,0:T(8,128)S(1)} custom-call(f32[16,16,3584]{2,1,0:T(8,128)} %bitcast.16, bf16[2,16,16,3584]{3,2,1,0:T(8,128)(2,1)} %bitcast.17, bf16[16,16,3584]{2,1,0:T(8,128)(2,1)} %bitcast.18, s32[16,3584]{1,0:T(8,128)} %water.1, s32[2,4,32]{2,1,0:T(4,128)} %bitcast.19, s32[1,32]{1,0:T(1,128)} %bitcast.21, ...), custom_call_target="tpu_custom_call" | custom-call | tf_op jit(solution)/shard_map/pallas_call | solution.py:714
  35.8 1.8 %shard_map.101 = f32[16,16,3584]{2,1,0:T(8,128)} custom-call(f32[16,16,3584]{2,1,0:T(8,128)S(1)} %shard_map.100.result), custom_call_target="tpu_custom_call" | custom-call | tf_op jit(solution)/shard_map/pallas_call | solution.py:763
